TPU v7x, 32 devices: a whole 2x2x4 slice. The times are simulated.
32 devices in a mesh: section: 4 (over x, core), expert: 8 (over z, y).
Axes of the slice: x: 2, y: 2, z: 4, core: 2. Of those that a mesh axis runs over, the one named last changes fastest.
Arguments:
- tokens: bfloat16 [2, 4, 512, 2048], P(None, 'section', 'expert'), may hold values from -24 to 24
- norm_gain: float32 [2048], replicated, may hold values from 0.1 to 1.9
- expert_ids: int32 [2, 4, 512, 2], P(None, 'section', 'expert'), may hold values from 0 to 11, all different within a row; in each aligned block of 64 rows (0 to 63, 64 to 127, ..., all dimensions but the last counted through in order) at most 11 rows name the same one
- route_scores: float32 [2, 4, 512, 2], P(None, 'section', 'expert'), may hold values from 0.1 to 1
- placement: int32 [32], replicated, may hold values from 0 to 11, as said below
- w_gate: bfloat16 [32, 2048, 768], P('expert'), as said below
- w_up: bfloat16 [32, 2048, 768], P('expert'), as said below
- w_down: bfloat16 [32, 768, 2048], P('expert'), as said below
Outputs:
- onward: bfloat16 [2, 4, 512, 2048], P(None, 'section', 'expert')
Inputs may be any that keep to these rules, and one draw needn't show every extreme that they name: `expert_ids`: in each micro-batch and section, the 64 rows of one device name each expert at most 11 times, a bound that some block reaches. `placement`: every expert holds two or more slots. `w_gate`: slots with equal placement hold equal gate projections. `w_up`: slots with equal placement hold equal up projections. `w_down`: slots with equal placement hold equal down projections.
All inputs are finite; a program needn't handle non-finite values.
Results may differ from a plain program's by a relative error of at most 0.0039.
Values may be sent and summed in bfloat16 or wider, within the bound.
A program may use at most 128 MiB of HBM per device.

v0:
```python
import jax
import jax.numpy as jnp
from jax import lax
from jax.sharding import PartitionSpec as P

EPSILON = 1e-06


def passed_along(x, axis, by):
    peers = lax.axis_size(axis)
    pairs = [(i, i + by) for i in range(peers) if 0 <= i + by < peers]
    return lax.ppermute(x, axis, pairs)


def normalize(rows, gain):
    values = rows.astype(jnp.float32)
    scale = lax.rsqrt(jnp.mean(values * values, axis=-1, keepdims=True) + EPSILON)
    return (values * scale * gain).astype(jnp.bfloat16)


def exclusive_rank(onehot):
    before = jnp.cumsum(onehot, axis=0) - onehot
    return jnp.sum(before * onehot, axis=1)


def route_rows(chosen, placement, experts, capacity):
    flat_ids = chosen.reshape(-1)
    slot_count = placement.shape[0]
    expert_range = jnp.arange(experts, dtype=jnp.int32)
    slot_range = jnp.arange(slot_count, dtype=jnp.int32)
    expert_hit = (flat_ids[:, None] == expert_range[None, :]).astype(jnp.int32)
    owner_hit = (placement[:, None] == expert_range[None, :]).astype(jnp.int32)
    replica_rank = exclusive_rank(owner_hit)
    copies = jnp.sum(owner_hit, axis=0)
    row_copies = jnp.sum(expert_hit * copies[None, :], axis=1)
    wanted = exclusive_rank(expert_hit) % row_copies
    matches = (placement[None, :] == flat_ids[:, None]) & (replica_rank[None, :] == wanted[:, None])
    target = jnp.sum(jnp.where(matches, slot_range[None, :], 0), axis=1)
    target_hit = (target[:, None] == slot_range[None, :]).astype(jnp.int32)
    position = exclusive_rank(target_hit)
    return (target * capacity + position).reshape(chosen.shape)


def body(tokens, norm_gain, expert_ids, route_scores, placement, w_gate, w_up, w_down):
    devices = lax.axis_size("expert")
    slot_dev = w_gate.shape[0]
    slot_count = placement.shape[0]
    experts = slot_count * 3 // 8
    tok_rows = tokens.shape[2]
    width = tokens.shape[3]
    chosen_count = expert_ids.shape[3]
    most_rows = (tok_rows * chosen_count + experts - 1) // experts
    capacity = (most_rows + 1) // 2
    buffer_range = jnp.arange(slot_count * capacity, dtype=jnp.int32)
    results = []
    for micro in range(2):
        prepare_rows = tokens[micro, 0]
        normed = normalize(prepare_rows, norm_gain)
        flat = route_rows(expert_ids[micro, 0], placement, experts, capacity)
        hits = flat[:, :, None] == buffer_range[None, None, :]
        take = jnp.any(hits, axis=1).astype(jnp.bfloat16)
        send = lax.dot_general(
            take, normed, (((0,), (0,)), ((), ())), preferred_element_type=jnp.float32
        )
        send = send.astype(jnp.bfloat16).reshape(devices, slot_dev, capacity, width)
        scores = route_scores[micro, 0]
        probs = scores / jnp.sum(scores, axis=1, keepdims=True)
        prepare_mixing = jnp.sum(jnp.where(hits, probs[:, :, None], 0.0), axis=1)
        rows, send, mixing = (prepare_rows, send, prepare_mixing)
        received = lax.all_to_all(send, "expert", split_axis=0, concat_axis=0, tiled=True)
        gate = jnp.einsum("sjcd,jdf->sjcf", received, w_gate, preferred_element_type=jnp.float32)
        up = jnp.einsum("sjcd,jdf->sjcf", received, w_up, preferred_element_type=jnp.float32)
        hidden = (jax.nn.silu(gate) * up).astype(jnp.bfloat16)
        returned = lax.all_to_all(
            jnp.einsum("sjcf,jfd->sjcd", hidden, w_down, preferred_element_type=jnp.float32).astype(
                jnp.bfloat16
            ),
            "expert",
            split_axis=0,
            concat_axis=0,
            tiled=True,
        )
        flat_back = returned.reshape(-1, width).astype(jnp.float32)
        moe = jnp.dot(
            mixing, flat_back, precision=lax.Precision.HIGHEST, preferred_element_type=jnp.float32
        )
        results.append((rows.astype(jnp.float32) + moe).astype(jnp.bfloat16))
    forward = passed_along(results[0], "section", 1)
    backward = passed_along(results[1], "section", -1)
    return jnp.stack([forward, backward], axis=0)[:, None]


def solution(mesh):
    in_specs = (
        P(None, "section", "expert", None),
        P(),
        P(None, "section", "expert", None),
        P(None, "section", "expert", None),
        P(),
        P("expert", None, None),
        P("expert", None, None),
        P("expert", None, None),
    )
    out_specs = P(None, "section", "expert", None)
    return jax.shard_map(body, mesh=mesh, in_specs=in_specs, out_specs=out_specs, check_vma=False)
```

profile of v0, /device:TPU:1, one launch (start us, length us, event | category | flops | bytes accessed | tf_op | source)
XLA Modules:
  0.0 124.4 jit_solution(10262340602217374018)
XLA Ops:
  0.0 0.7 fusion.88
  0.8 0.1 eq.78
  1.1 0.1 eq.180
  1.4 0.2 reduce_window_sum.47
  1.5 0.2 reduce_window_sum.49
  1.7 0.7 fusion.84
  2.5 0.8 fusion.85
  3.3 0.2 select_reduce_fusion.8
  3.6 0.1 and_select_fusion
  3.7 0.9 select_reduce_fusion.7
  4.7 0.2 reduce_window_sum.48
  4.8 0.2 select_reduce_fusion.6
  5.0 0.1 add.66
  5.2 0.1 fusion.79
  5.4 1.2 fusion.54
  6.6 1.4 %convolution_convert_fusion.1 = bf16[192,2048]{1,0:T(8,128)(2,1)S(1)} fusion(pred[64,192]{1,0:T(8,128)(4,1)S(1)} %fusion.79, f32[2048]{0:T(1024)} %param.9, f32[64]{0:T(128)S(1)} %get-tuple-element.24, bf16[2,1,64,2048]{3,2,1,0:T(8,128)(2,1)} %param.8), kind=kOutput, calls=%fused_computation.15 | convolution fusion | flops 51249152 | bytes 1069312 | tf_op jit(solution)/shard_map/dot_general | solution.py:62
  8.0 0.3 reshape.135
  8.3 1.5 %copy.53 = bf16[8,4,6,2048]{3,1,2,0:T(4,128)(2,1)} copy(bf16[8,4,6,2048]{3,2,1,0:T(8,128)(2,1)S(1)} %reshape.135) | data formatting | bytes 1572864 | tf_op jit(solution)/shard_map/reshape | solution.py:65
  9.8 6.4 %all-to-all-start = ((bf16[8,4,6,2048]{3,1,2,0:T(4,128)(2,1)}), bf16[8,4,6,2048]{3,1,2,0:T(4,128)(2,1)S(1)}, u32[]{:S(2)}, u32[]{:S(2)}) async-start(bf16[8,4,6,2048]{3,1,2,0:T(4,128)(2,1)} %copy.53), calls=%async_computation | async-start | bytes 1572864 | tf_op jit(solution)/shard_map/all_to_all | solution.py:70
  16.3 0.2 reduce_window_sum.50
  16.5 0.2 select_reduce_fusion.2
  16.6 0.1 add.72
  16.9 0.1 fusion.78
  17.0 1.4 %convolution_convert_fusion = bf16[192,2048]{1,0:T(8,128)(2,1)S(1)} fusion(pred[64,192]{1,0:T(8,128)(4,1)S(1)} %fusion.78, f32[64]{0:T(128)S(1)} %get-tuple-element.23, f32[2048]{0:T(1024)} %param.9, bf16[2,1,64,2048]{3,2,1,0:T(8,128)(2,1)} %param.8), kind=kOutput, calls=%fused_computation.14 | convolution fusion | flops 51249152 | bytes 1069312 | tf_op jit(solution)/shard_map/dot_general | solution.py:62
  18.4 0.3 reshape.137
  18.7 1.5 %copy.60 = bf16[8,4,6,2048]{3,1,2,0:T(4,128)(2,1)} copy(bf16[8,4,6,2048]{3,2,1,0:T(8,128)(2,1)S(1)} %reshape.137) | data formatting | bytes 1572864 | tf_op jit(solution)/shard_map/reshape | solution.py:65
  20.1 15.1 %all-to-all-done = bf16[8,4,6,2048]{3,1,2,0:T(4,128)(2,1)S(1)} async-done(((bf16[8,4,6,2048]{3,1,2,0:T(4,128)(2,1)}), bf16[8,4,6,2048]{3,1,2,0:T(4,128)(2,1)S(1)}, u32[]{:S(2)}, u32[]{:S(2)}) %all-to-all-start) | async-done | bytes 786464 | tf_op jit(solution)/shard_map/all_to_all | solution.py:70
  35.3 4.9 %all-to-all-start.2 = ((bf16[8,4,6,2048]{3,1,2,0:T(4,128)(2,1)}), bf16[8,4,6,2048]{3,1,2,0:T(4,128)(2,1)S(1)}, u32[]{:S(2)}, u32[]{:S(2)}) async-start(bf16[8,4,6,2048]{3,1,2,0:T(4,128)(2,1)} %copy.60), calls=%async_computation.2 | async-start | bytes 1572864 | tf_op jit(solution)/shard_map/all_to_all | solution.py:70
  40.1 7.1 %fusion.26 = f32[8,4,6,768]{3,0,2,1:T(8,128)S(1)} fusion(bf16[4,2048,768]{2,1,0:T(8,128)(2,1)} %param.13, bf16[8,4,6,2048]{3,1,2,0:T(4,128)(2,1)S(1)} %all-to-all-done), kind=kOutput, calls=%fused_computation.22 | convolution fusion | flops 603979776 | bytes 13959168 | tf_op jit(solution)/shard_map/sjcd,jdf->sjcf/dot_general | solution.py:71
  47.2 12.9 %fusion.21 = bf16[8,4,6,2048]{3,0,2,1:T(8,128)(2,1)S(1)} fusion(bf16[4,768,2048]{2,1,0:T(8,128)(2,1)} %param.15, bf16[4,2048,768]{2,1,0:T(8,128)(2,1)} %param.14, bf16[8,4,6,2048]{3,1,2,0:T(4,128)(2,1)S(1)} %all-to-all-done, f32[8,4,6,768]{3,0,2,1:T(8,128)S(1)} %fusion.26), kind=kOutput, calls=%fused_computation.17 | convolution fusion | flops 1209237504 | bytes 27328512 | tf_op jit(solution)/shard_map/sjcf,jfd->sjcd/dot_general | solution.py:75
  60.1 1.5 %copy.56 = bf16[8,4,6,2048]{3,1,2,0:T(4,128)(2,1)} copy(bf16[8,4,6,2048]{3,0,2,1:T(8,128)(2,1)S(1)} %fusion.21) | data formatting | bytes 1572864 | tf_op jit(solution)/shard_map/convert_element_type | solution.py:75
  61.6 5.4 %all-to-all-start.1 = ((bf16[8,4,6,2048]{3,1,2,0:T(4,128)(2,1)}), bf16[8,4,6,2048]{3,1,2,0:T(4,128)(2,1)S(1)}, u32[]{:S(2)}, u32[]{:S(2)}) async-start(bf16[8,4,6,2048]{3,1,2,0:T(4,128)(2,1)} %copy.56), calls=%async_computation.1 | async-start | bytes 1572864 | tf_op jit(solution)/shard_map/all_to_all | solution.py:74
  67.0 7.1 %fusion.29 = f32[8,4,6,768]{3,0,2,1:T(8,128)S(1)} fusion(bf16[4,2048,768]{2,1,0:T(8,128)(2,1)} %param.13, bf16[8,4,6,2048]{3,1,2,0:T(4,128)(2,1)S(1)} %all-to-all-done.2), kind=kOutput, calls=%fused_computation.23 | convolution fusion | flops 603979776 | bytes 13959168 | tf_op jit(solution)/shard_map/sjcd,jdf->sjcf/dot_general | solution.py:71
  74.1 12.9 %fusion.18 = bf16[8,4,6,2048]{3,0,2,1:T(8,128)(2,1)S(1)} fusion(bf16[4,768,2048]{2,1,0:T(8,128)(2,1)} %param.15, bf16[4,2048,768]{2,1,0:T(8,128)(2,1)} %param.14, bf16[8,4,6,2048]{3,1,2,0:T(4,128)(2,1)S(1)} %all-to-all-done.2, f32[8,4,6,768]{3,0,2,1:T(8,128)S(1)} %fusion.29), kind=kOutput, calls=%fused_computation.16 | convolution fusion | flops 1209237504 | bytes 27328512 | tf_op jit(solution)/shard_map/sjcf,jfd->sjcd/dot_general | solution.py:75
  87.1 1.5 %copy.63 = bf16[8,4,6,2048]{3,1,2,0:T(4,128)(2,1)} copy(bf16[8,4,6,2048]{3,0,2,1:T(8,128)(2,1)S(1)} %fusion.18) | data formatting | bytes 1572864 | tf_op jit(solution)/shard_map/convert_element_type | solution.py:75
  88.6 5.4 %all-to-all-start.3 = ((bf16[8,4,6,2048]{3,1,2,0:T(4,128)(2,1)}), bf16[8,4,6,2048]{3,1,2,0:T(4,128)(2,1)S(1)}, u32[]{:S(2)}, u32[]{:S(2)}) async-start(bf16[8,4,6,2048]{3,1,2,0:T(4,128)(2,1)} %copy.63), calls=%async_computation.3 | async-start | bytes 1572864 | tf_op jit(solution)/shard_map/all_to_all | solution.py:74
  94.0 0.1 select_reduce_fusion.1
  94.3 0.5 copy.57
  94.7 0.3 reshape.136
  95.0 1.2 fusion.24
  96.2 4.9 %collective-permute-start = (bf16[64,2048]{1,0:T(8,128)(2,1)}, bf16[64,2048]{1,0:T(8,128)(2,1)S(1)}, u32[]{:S(2)}, u32[]{:S(2)}) collective-permute-start(bf16[64,2048]{1,0:T(8,128)(2,1)} %fusion.24), channel_id=1, source_target_pairs={{0,8},{8,16},{16,24},{1,9},{9,17},{17,25},{2,10},{10,18},{18,26},{... | collective-permute-start | bytes 786440 | tf_op jit(solution)/shard_map/ppermute | solution.py:12
  101.1 11.3 %all-to-all-done.3 = bf16[8,4,6,2048]{3,1,2,0:T(4,128)(2,1)S(1)} async-done(((bf16[8,4,6,2048]{3,1,2,0:T(4,128)(2,1)}), bf16[8,4,6,2048]{3,1,2,0:T(4,128)(2,1)S(1)}, u32[]{:S(2)}, u32[]{:S(2)}) %all-to-all-start.3) | async-done | bytes 786464 | tf_op jit(solution)/shard_map/all_to_all | solution.py:74
  112.4 0.5 copy.64
  112.8 0.3 reshape.138
  113.1 0.5 fusion.25
  113.7 4.7 %collective-permute-start.1 = (bf16[64,2048]{1,0:T(8,128)(2,1)S(1)}, bf16[64,2048]{1,0:T(8,128)(2,1)S(1)}, u32[]{:S(2)}, u32[]{:S(2)}) collective-permute-start(bf16[64,2048]{1,0:T(8,128)(2,1)S(1)} %fusion.25), channel_id=1, source_target_pairs={{8,0},{16,8},{24,16},{9,1},{17,9},{25,17},{10,2},{18,10},{26,18},{... | collective-permute-start | bytes 786440 | tf_op jit(solution)/shard_map/ppermute | solution.py:12
  118.4 5.1 %collective-permute-done.1 = bf16[64,2048]{1,0:T(8,128)(2,1)S(1)} collective-permute-done((bf16[64,2048]{1,0:T(8,128)(2,1)S(1)}, bf16[64,2048]{1,0:T(8,128)(2,1)S(1)}, u32[]{:S(2)}, u32[]{:S(2)}) %collective-permute-start.1) | collective-permute-done | bytes 262176 | tf_op jit(solution)/shard_map/ppermute | solution.py:12
  123.5 0.8 maximum_bitcast_fusion
  (22 shorter events, 0.9 us)
Async XLA Ops:
  9.8 25.4 %all-to-all-start = ((bf16[8,4,6,2048]{3,1,2,0:T(4,128)(2,1)}), bf16[8,4,6,2048]{3,1,2,0:T(4,128)(2,1)S(1)}, u32[]{:S(2)}, u32[]{:S(2)}) async-start(bf16[8,4,6,2048]{3,1,2,0:T(4,128)(2,1)} %copy.53), calls=%async_computation | async-start | bytes 1572864 | tf_op jit(solution)/shard_map/all_to_all | solution.py:70
  35.3 26.3 %all-to-all-start.2 = ((bf16[8,4,6,2048]{3,1,2,0:T(4,128)(2,1)}), bf16[8,4,6,2048]{3,1,2,0:T(4,128)(2,1)S(1)}, u32[]{:S(2)}, u32[]{:S(2)}) async-start(bf16[8,4,6,2048]{3,1,2,0:T(4,128)(2,1)} %copy.60), calls=%async_computation.2 | async-start | bytes 1572864 | tf_op jit(solution)/shard_map/all_to_all | solution.py:70
  61.6 27.0 %all-to-all-start.1 = ((bf16[8,4,6,2048]{3,1,2,0:T(4,128)(2,1)}), bf16[8,4,6,2048]{3,1,2,0:T(4,128)(2,1)S(1)}, u32[]{:S(2)}, u32[]{:S(2)}) async-start(bf16[8,4,6,2048]{3,1,2,0:T(4,128)(2,1)} %copy.56), calls=%async_computation.1 | async-start | bytes 1572864 | tf_op jit(solution)/shard_map/all_to_all | solution.py:74
  74.1 19.9 %copy-start.1 = (f32[2,1,64,2]{2,3,1,0:T(2,128)S(1)}, f32[2,1,64,2]{2,3,1,0:T(2,128)}, u32[]{:S(2)}) copy-start(f32[2,1,64,2]{2,3,1,0:T(2,128)} %param.11) | copy-start | bytes 3076
  74.1 20.9 %copy-start = (bf16[2,1,64,2048]{3,2,1,0:T(8,128)(2,1)S(1)}, bf16[2,1,64,2048]{3,2,1,0:T(8,128)(2,1)}, u32[]{:S(2)}) copy-start(bf16[2,1,64,2048]{3,2,1,0:T(8,128)(2,1)} %param.8) | copy-start | bytes 1572868
  88.6 23.8 %all-to-all-start.3 = ((bf16[8,4,6,2048]{3,1,2,0:T(4,128)(2,1)}), bf16[8,4,6,2048]{3,1,2,0:T(4,128)(2,1)S(1)}, u32[]{:S(2)}, u32[]{:S(2)}) async-start(bf16[8,4,6,2048]{3,1,2,0:T(4,128)(2,1)} %copy.63), calls=%async_computation.3 | async-start | bytes 1572864 | tf_op jit(solution)/shard_map/all_to_all | solution.py:74
  96.2 22.1 %collective-permute-start = (bf16[64,2048]{1,0:T(8,128)(2,1)}, bf16[64,2048]{1,0:T(8,128)(2,1)S(1)}, u32[]{:S(2)}, u32[]{:S(2)}) collective-permute-start(bf16[64,2048]{1,0:T(8,128)(2,1)} %fusion.24), channel_id=1, source_target_pairs={{0,8},{8,16},{16,24},{1,9},{9,17},{17,25},{2,10},{10,18},{18,26},{... | collective-permute-start | bytes 786440 | tf_op jit(solution)/shard_map/ppermute | solution.py:12
  113.7 9.9 %collective-permute-start.1 = (bf16[64,2048]{1,0:T(8,128)(2,1)S(1)}, bf16[64,2048]{1,0:T(8,128)(2,1)S(1)}, u32[]{:S(2)}, u32[]{:S(2)}) collective-permute-start(bf16[64,2048]{1,0:T(8,128)(2,1)S(1)} %fusion.25), channel_id=1, source_target_pairs={{8,0},{16,8},{24,16},{9,1},{17,9},{25,17},{10,2},{18,10},{26,18},{... | collective-permute-start | bytes 786440 | tf_op jit(solution)/shard_map/ppermute | solution.py:12
where the time goes:
time: 125 us; the launch traced here: 124 us
  matrix products  44.5 us (36%)
  starting transfers between devices  31.7 us (25%)
  waiting for transfers between devices  31.5 us (25%)
  local copies, waits for them, and re-layouts  9.57 us (8%)
  other arithmetic  6.75 us (5%)
    dot_general x2, matrix products, body(): jnp.einsum('sjcf,jfd->sjcd', hidden, w_down, preferred_element_type=jnp.f...  25.8 us
    all_to_all x2, waiting for transfers between devices, body(): lax.all_to_all(send, 'expert', split_axis=0, concat_axis=0, tiled=True)  15.1 us
    dot_general x2, matrix products, body(): jnp.einsum('sjcd,jdf->sjcf', received, w_gate, preferred_element_type=jnp...  14.1 us
    all_to_all x2, starting transfers between devices, body(): lax.all_to_all(send, 'expert', split_axis=0, concat_axis=0, tiled=True)  11.3 us
    all_to_all x2, waiting for transfers between devices, body(): lax.all_to_all(jnp.einsum('sjcf,jfd->sjcd', hidden, w_down, preferred_ele...  11.3 us
    all_to_all x2, starting transfers between devices, body(): lax.all_to_all(jnp.einsum('sjcf,jfd->sjcd', hidden, w_down, preferred_ele...  10.9 us
    ppermute x2, starting transfers between devices, passed_along(): return lax.ppermute(x, axis, pairs)  9.61 us
    ppermute x2, waiting for transfers between devices, passed_along(): return lax.ppermute(x, axis, pairs)  5.13 us
  transfers between devices with their start and end apart: 6, of which 3 were waited for; matrix products, arithmetic and copies ran while one was open for 40% of the time, Pallas kernels for 0%

commit v1 on v0

v1 whole, which is shorter than its diff:
```python
import functools

import jax
import jax.numpy as jnp
from jax import lax
from jax.experimental import pallas as pl
from jax.experimental.pallas import tpu as pltpu
from jax.sharding import PartitionSpec as P

EPSILON = 1e-06
STRIDE = 1024
MARK = 1 << 20
MESH = pl.DeviceIdType.MESH
COLUMNS = 256


def round_up(value, to):
    return (value + to - 1) // to * to


def split_columns(width):
    return COLUMNS if width % COLUMNS == 0 else width


def layer(
    near, far, slots,
    tokens, gain, ids, scores, code_near, code_far, slot_near, slot_far, w_gate, w_up, w_down,
    out,
    gate_buf, up_buf, down_buf, normed, hits_near, hits_far, hidden, mixed,
    send_n, send_f, recv_n, recv_f, done_n, done_f, back_n, back_f,
    weight_sem, to_n, from_n, to_f, from_f, ret_to_n, ret_from_n, ret_to_f, ret_from_f, relay_to, relay_from,
):
    section = lax.axis_index("section")
    sections = lax.axis_size("section")
    me = lax.axis_index("expert")
    peers = lax.axis_size("expert")
    half = peers // 2
    mine = me % half
    side = me // half
    micros, rows, width = tokens.shape
    top = ids.shape[2]
    experts = STRIDE

    loads = []
    for slot in range(slots):
        for kind, (src, dst) in enumerate(((w_gate, gate_buf), (w_up, up_buf), (w_down, down_buf))):
            copy = pltpu.make_async_copy(src.at[slot], dst.at[slot], weight_sem.at[kind, slot])
            copy.start()
            loads.append(copy)

    barrier = pltpu.get_barrier_semaphore()

    def greet(step, carry):
        pl.semaphore_signal(
            barrier, inc=1, device_id=(section, (me + step) % peers), device_id_type=MESH
        )
        return carry

    lax.fori_loop(1, peers, greet, 0)

    @pl.when(section > 0)
    def _():
        pl.semaphore_signal(barrier, inc=1, device_id=(section - 1, me), device_id_type=MESH)

    @pl.when(section < sections - 1)
    def _():
        pl.semaphore_signal(barrier, inc=1, device_id=(section + 1, me), device_id_type=MESH)

    lane = lax.broadcasted_iota(jnp.int32, (rows, 128), 1)
    lower = (
        lax.broadcasted_iota(jnp.int32, (rows, rows), 0)
        > lax.broadcasted_iota(jnp.int32, (rows, rows), 1)
    ).astype(jnp.bfloat16)
    mixing = []
    for micro in range(micros):
        values = tokens[micro].astype(jnp.float32)
        scale = lax.rsqrt(jnp.mean(values * values, axis=-1, keepdims=True) + EPSILON)
        normed[micro] = (values * scale * gain[...]).astype(jnp.bfloat16)
        ones = [(ids[micro][:, k : k + 1] == lane).astype(jnp.float32) for k in range(top)]
        both = functools.reduce(jnp.add, ones)
        before = jnp.dot(lower, both.astype(jnp.bfloat16), preferred_element_type=jnp.float32)
        chosen = scores[micro]
        probs = chosen / jnp.sum(chosen, axis=1, keepdims=True)
        take_n = take_f = mix_n = mix_f = 0.0
        for k in range(top):
            rank = jnp.sum(before * ones[k], axis=1, keepdims=True).astype(jnp.int32)
            code = ids[micro][:, k : k + 1] * STRIDE + rank
            in_n = (code == code_near[...]).astype(jnp.float32)
            in_f = (code + micro * MARK == code_far[...]).astype(jnp.float32)
            take_n = take_n + in_n
            take_f = take_f + in_f
            mix_n = mix_n + in_n * probs[:, k : k + 1]
            mix_f = mix_f + in_f * probs[:, k : k + 1]
        hits_near[micro] = take_n.astype(jnp.bfloat16)
        hits_far[micro] = take_f.astype(jnp.bfloat16)
        mixing.append((mix_n, mix_f))

    def gather(hits, source):
        return lax.dot_general(
            hits, source, (((0,), (0,)), ((), ())), preferred_element_type=jnp.float32
        )

    send_f[...] = (
        sum(gather(hits_far[micro], normed[micro]) for micro in range(micros))
        .astype(jnp.bfloat16)
        .reshape(send_f.shape)
    )

    greeted = (
        peers - 1 + (section > 0).astype(jnp.int32) + (section < sections - 1).astype(jnp.int32)
    )
    pl.semaphore_wait(barrier, greeted)

    def far_copy(step, src, dst, sent, arrived):
        there = (mine + step) % half
        return pltpu.make_async_remote_copy(
            src_ref=src.at[there],
            dst_ref=dst.at[mine],
            send_sem=sent.at[step],
            recv_sem=arrived.at[step],
            device_id=(section, (1 - side) * half + there),
            device_id_type=MESH,
        )

    def near_copy(micro, step, src, dst, sent, arrived):
        there = (mine + step) % half
        return pltpu.make_async_remote_copy(
            src_ref=src.at[micro, there],
            dst_ref=dst.at[micro, mine],
            send_sem=sent.at[micro, step],
            recv_sem=arrived.at[micro, step],
            device_id=(section, side * half + there),
            device_id_type=MESH,
        )

    def each(first, act):
        def step_body(step, carry):
            act(step)
            return carry

        lax.fori_loop(first, half, step_body, 0)

    each(0, lambda step: far_copy(step, send_f, recv_f, to_f, from_f).start())
    for micro in range(micros):
        send_n[micro] = (
            gather(hits_near[micro], normed[micro]).astype(jnp.bfloat16).reshape(send_n.shape[1:])
        )
        each(1, lambda step: near_copy(micro, step, send_n, recv_n, to_n, from_n).start())
        recv_n[micro, mine] = send_n[micro, mine]

    def experts_of(count, inputs, owner, store):
        ff = gate_buf.shape[2]
        block = split_columns(ff)
        per = ff // block

        def up_body(step, carry):
            slot = step // per
            cols = pl.ds(pl.multiple_of((step % per) * block, block), block)
            x = inputs()
            gate = jnp.dot(x, gate_buf[slot, :, cols], preferred_element_type=jnp.float32)
            up = jnp.dot(x, up_buf[slot, :, cols], preferred_element_type=jnp.float32)
            unit = gate / (1.0 + jnp.exp(-gate)) * up
            unit = jnp.where(owner == slot, unit, 0.0)
            hidden[step, :count] = unit.astype(jnp.bfloat16)
            return carry

        lax.fori_loop(0, slots * per, up_body, 0)
        wide = split_columns(width)

        def down_body(step, carry):
            cols = pl.ds(pl.multiple_of(step * wide, wide), wide)
            total = jnp.zeros((count, wide), jnp.float32)
            for slot in range(slots):
                for part in range(per):
                    total = total + jnp.dot(
                        hidden[slot * per + part, :count],
                        down_buf[slot, part * block : (part + 1) * block, cols],
                        preferred_element_type=jnp.float32,
                    )
            store(cols, total.astype(jnp.bfloat16))
            return carry

        lax.fori_loop(0, width // wide, down_body, 0)

    rows_n, rows_f = half * near, half * far * micros

    each(0, lambda step: far_copy(step, send_f, recv_f, to_f, from_f).wait_recv())
    each(1, lambda step: near_copy(0, step, send_n, recv_n, to_n, from_n).wait_recv())
    for copy in loads:
        copy.wait()

    def store_first(cols, value):
        done_f[:, :, cols] = value[:rows_f].reshape(half, far * micros, value.shape[1])
        done_n[0, :, :, cols] = value[rows_f:].reshape(half, near, value.shape[1])

    experts_of(
        rows_f + rows_n,
        lambda: jnp.concatenate(
            [recv_f[...].reshape(rows_f, width), recv_n[0].reshape(rows_n, width)], axis=0
        ),
        jnp.concatenate([slot_far[...], slot_near[...]], axis=0),
        store_first,
    )
    each(0, lambda step: far_copy(step, done_f, back_f, ret_to_f, ret_from_f).start())
    each(1, lambda step: near_copy(0, step, done_n, back_n, ret_to_n, ret_from_n).start())
    back_n[0, mine] = done_n[0, mine]

    for micro in range(1, micros):
        each(1, lambda step: near_copy(micro, step, send_n, recv_n, to_n, from_n).wait_recv())

        def store_next(cols, value):
            done_n[micro, :, :, cols] = value.reshape(half, near, value.shape[1])

        experts_of(
            rows_n, lambda: recv_n[micro].reshape(rows_n, width), slot_near[...], store_next
        )
        each(1, lambda step: near_copy(micro, step, done_n, back_n, ret_to_n, ret_from_n).start())
        back_n[micro, mine] = done_n[micro, mine]

    def weighed(mix, values):
        high = mix.astype(jnp.bfloat16)
        low = (mix - high.astype(jnp.float32)).astype(jnp.bfloat16)
        return jnp.dot(high, values, preferred_element_type=jnp.float32) + jnp.dot(
            low, values, preferred_element_type=jnp.float32
        )

    def relay(micro, by):
        return pltpu.make_async_remote_copy(
            src_ref=mixed.at[micro],
            dst_ref=out.at[micro],
            send_sem=relay_to.at[micro],
            recv_sem=relay_from.at[micro],
            device_id=(section + by, me),
            device_id_type=MESH,
        )

    each(0, lambda step: far_copy(step, done_f, back_f, ret_to_f, ret_from_f).wait_recv())
    sends = ((0, 1, section < sections - 1, section > 0), (1, -1, section > 0, section < sections - 1))
    for micro, by, gives, gets in sends:
        each(1, lambda step: near_copy(micro, step, done_n, back_n, ret_to_n, ret_from_n).wait_recv())
        mix_n, mix_f = mixing[micro]
        total = tokens[micro].astype(jnp.float32)
        total = total + weighed(mix_f, back_f[...].reshape(rows_f, width))
        total = total + weighed(mix_n, back_n[micro].reshape(rows_n, width))
        mixed[micro] = total.astype(jnp.bfloat16)

        @pl.when(gives)
        def _():
            relay(micro, by).start()

        @pl.when(jnp.logical_not(gets))
        def _():
            out[micro] = jnp.zeros(out.shape[1:], out.dtype)

    each(0, lambda step: far_copy(step, send_f, recv_f, to_f, from_f).wait_send())
    each(0, lambda step: far_copy(step, done_f, back_f, ret_to_f, ret_from_f).wait_send())
    for micro in range(micros):
        each(1, lambda step: near_copy(micro, step, send_n, recv_n, to_n, from_n).wait_send())
        each(1, lambda step: near_copy(micro, step, done_n, back_n, ret_to_n, ret_from_n).wait_send())
    for micro, by, gives, gets in sends:

        @pl.when(gives)
        def _():
            relay(micro, by).wait_send()

        @pl.when(gets)
        def _():
            relay(micro, by).wait_recv()


def places(placement, devices, slot_cap, near, far):
    slots = placement.shape[0]
    slot_range = jnp.arange(slots, dtype=jnp.int32)
    same = placement[:, None] == placement[None, :]
    copies = jnp.sum(same, axis=1, dtype=jnp.int32)
    replica = jnp.sum(same & (slot_range[None, :] < slot_range[:, None]), axis=1, dtype=jnp.int32)
    index = jnp.arange(slot_cap, dtype=jnp.int32)
    code = placement[:, None] * STRIDE + index[None, :] * copies[:, None] + replica[:, None]
    per = slots // devices
    code = code.reshape(devices, per * slot_cap)
    owner = jnp.broadcast_to(jnp.arange(per, dtype=jnp.int32)[:, None], (per, slot_cap)).reshape(-1)
    fill_n, fill_f = near - per * slot_cap, far - per * slot_cap
    code_n = jnp.pad(code, ((0, 0), (0, fill_n)), constant_values=-1)
    code_f = jnp.pad(code, ((0, 0), (0, fill_f)), constant_values=-1)
    return code_n, code_f, jnp.pad(owner, (0, fill_n)), jnp.pad(owner, (0, fill_f))


def body(tokens, norm_gain, expert_ids, route_scores, placement, w_gate, w_up, w_down):
    devices = lax.axis_size("expert")
    half = devices // 2
    side = lax.axis_index("expert") // half
    slots = w_gate.shape[0]
    ff = w_gate.shape[2]
    micros, _, rows, width = tokens.shape
    top = expert_ids.shape[3]
    experts = placement.shape[0] * 3 // 8
    most = (rows * top + experts - 1) // experts
    slot_cap = (most + 1) // 2
    near = round_up(slots * slot_cap, 16)
    far = round_up(slots * slot_cap, 8)
    code_n, code_f, owner_n, owner_f = places(placement, devices, slot_cap, near, far)

    code_near = lax.dynamic_slice_in_dim(code_n, side * half, half, 0).reshape(1, half * near)
    code_there = lax.dynamic_slice_in_dim(code_f, (1 - side) * half, half, 0)
    marks = jnp.arange(micros, dtype=jnp.int32) * MARK
    code_far = jnp.where(
        code_there[:, None, :] >= 0, code_there[:, None, :] + marks[None, :, None], -1
    ).reshape(1, half * micros * far)
    slot_near = jnp.broadcast_to(owner_n[None, :], (half, near)).reshape(half * near, 1)
    slot_far = jnp.broadcast_to(owner_f[None, None, :], (half, micros, far)).reshape(-1, 1)

    rows_n, rows_f = half * near, half * micros * far
    vmem = pl.BlockSpec(memory_space=pltpu.VMEM)
    block = split_columns(ff)
    n_shape = (micros, half, near, width)
    f_shape = (half, micros * far, width)
    bf16 = jnp.bfloat16
    dma = pltpu.SemaphoreType.DMA
    result = pl.pallas_call(
        functools.partial(layer, near, far, slots),
        out_shape=jax.ShapeDtypeStruct((micros, rows, width), bf16),
        in_specs=[vmem] * 8 + [pl.BlockSpec(memory_space=pl.ANY)] * 3,
        out_specs=vmem,
        scratch_shapes=[
            pltpu.VMEM(w_gate.shape, bf16),
            pltpu.VMEM(w_up.shape, bf16),
            pltpu.VMEM(w_down.shape, bf16),
            pltpu.VMEM((micros, rows, width), bf16),
            pltpu.VMEM((micros, rows, rows_n), bf16),
            pltpu.VMEM((micros, rows, rows_f), bf16),
            pltpu.VMEM((slots * (ff // block), rows_n + rows_f, block), bf16),
            pltpu.VMEM((micros, rows, width), bf16),
            pltpu.VMEM(n_shape, bf16),
            pltpu.VMEM(f_shape, bf16),
            pltpu.VMEM(n_shape, bf16),
            pltpu.VMEM(f_shape, bf16),
            pltpu.VMEM(n_shape, bf16),
            pltpu.VMEM(f_shape, bf16),
            pltpu.VMEM(n_shape, bf16),
            pltpu.VMEM(f_shape, bf16),
            dma((3, slots)),
            dma((micros, half)),
            dma((micros, half)),
            dma((half,)),
            dma((half,)),
            dma((micros, half)),
            dma((micros, half)),
            dma((half,)),
            dma((half,)),
            dma((micros,)),
            dma((micros,)),
        ],
        compiler_params=pltpu.CompilerParams(
            collective_id=0, has_side_effects=True, vmem_limit_bytes=62 << 20
        ),
    )(
        tokens[:, 0], norm_gain[None, :], expert_ids[:, 0], route_scores[:, 0],
        code_near, code_far, slot_near, slot_far, w_gate, w_up, w_down,
    )
    return result[:, None]


def solution(mesh):
    in_specs = (
        P(None, "section", "expert", None),
        P(),
        P(None, "section", "expert", None),
        P(None, "section", "expert", None),
        P(),
        P("expert", None, None),
        P("expert", None, None),
        P("expert", None, None),
    )
    out_specs = P(None, "section", "expert", None)
    return jax.shard_map(body, mesh=mesh, in_specs=in_specs, out_specs=out_specs, check_vma=False)
```

time: 125 us -> 107 us (0.86)
  Pallas kernels: 0 us -> 96.2 us
  matrix products: 44.5 us -> 0 us
  starting transfers between devices: 31.7 us -> 0 us
  waiting for transfers between devices: 31.5 us -> 0 us
  other arithmetic: 6.75 us -> 1.66 us
  local copies, waits for them, and re-layouts: 9.57 us -> 8.31 us
    pallas_call x0 -> x1, Pallas kernels: none -> 96.2 us  [body(): pl.pallas_call(functools.partial(layer, near, far, slots), out_shape=jax....]
    dot_general x8 -> x0, matrix products: 44.5 us -> none  [the longest x2 25.8 us: body(): jnp.einsum('sjcf,jfd->sjcd', hidden, w_down, preferred_element_type=jnp.f...]
    all_to_all x4 -> x0, waiting for transfers between devices: 26.4 us -> none  [the longest x2 15.1 us: body(): lax.all_to_all(send, 'expert', split_axis=0, concat_axis=0, tiled=True)]
    all_to_all x4 -> x0, starting transfers between devices: 22.1 us -> none  [the longest x2 11.3 us: body(): lax.all_to_all(send, 'expert', split_axis=0, concat_axis=0, tiled=True)]
    ppermute x2 -> x0, starting transfers between devices: 9.61 us -> none  [passed_along(): return lax.ppermute(x, axis, pairs)]
    ppermute x2 -> x0, waiting for transfers between devices: 5.13 us -> none  [passed_along(): return lax.ppermute(x, axis, pairs)]
    unnamed x4 -> x3, local copies, waits for them, and re-layouts: 0.01 us -> 4.69 us
    convert_element_type x2 -> x0, local copies, waits for them, and re-layouts: 3 us -> none  [body(): jnp.einsum('sjcf,jfd->sjcd', hidden, w_down, preferred_element_type=jnp.f...]
  transfers between devices with their start and end apart: 6 -> 0, of which waited for: 3 -> 0; matrix products, arithmetic and copies ran while one was open for 40% -> 0% of each run, Pallas kernels for 0% -> 0%
where the time goes in v1:
time: 107 us; the launch traced here: 106 us
  Pallas kernels  96.2 us (90%)
  local copies, waits for them, and re-layouts  8.31 us (8%)
  other arithmetic  1.66 us (2%)
    pallas_call x1, Pallas kernels, body(): pl.pallas_call(functools.partial(layer, near, far, slots), out_shape=jax....  96.2 us
    unnamed x3, local copies, waits for them, and re-layouts  4.69 us

profile of v1, /device:TPU:1, one launch (start us, length us, event | category | flops | bytes accessed | tf_op | source)
XLA Modules:
  0.0 106.2 jit_solution(15514281241210073829)
XLA Ops:
  0.0 0.7 broadcast_multiply_fusion
  0.7 0.9 fusion
  1.6 0.1 reshape.79
  1.7 0.1 mul.45
  1.8 0.1 mul.47
  1.8 0.1 add.58
  1.9 0.1 add.62
  2.0 0.1 add.63
  2.1 0.1 add.64
  2.2 0.1 add.59
  2.2 0.1 add.60
  2.3 0.1 mul.48
  2.4 0.1 mul.49
  2.5 0.6 reshape.78.code_near
  3.1 0.1 add_select_fusion
  3.2 0.6 select_n.29.code_far
  3.8 0.7 reshape.82.slot_near
  4.6 1.4 %copy.18 = s32[2,1,64,2]{3,2,0,1:T(8,128)} copy(s32[2,1,64,2]{2,3,1,0:T(2,128)} %param.10) | data formatting | bytes 2048 | tf_op args[2]
  6.0 1.4 %copy.19 = f32[2,1,64,2]{3,2,0,1:T(8,128)} copy(f32[2,1,64,2]{2,3,1,0:T(2,128)} %param.11) | data formatting | bytes 2048 | tf_op args[3]
  7.4 0.7 reshape.83.slot_far
  8.1 96.2 %shard_map.82 = bf16[2,64,2048]{2,1,0:T(8,128)(2,1)} custom-call(bf16[2,64,2048]{2,1,0:T(8,128)(2,1)} %bitcast.8, f32[1,2048]{1,0:T(1,128)} %bitcast.11, s32[2,64,2]{2,1,0:T(8,128)} %bitcast.9, f32[2,64,2]{2,1,0:T(8,128)} %bitcast.10, s32[1,128]{1,0:T(1,128)} %reshape.78.code_near, s32[1,192]{1,0:T(1,128)} %select_n.29.code_far, ...), custom_call_target="tpu_custom_call" | custom-call | tf_op jit(solution)/shard_map/pallas_call | solution.py:319
  104.3 1.9 %copy.24 = bf16[2,1,64,2048]{3,2,1,0:T(8,128)(2,1)} copy(bf16[2,1,64,2048]{3,2,1,0:T(8,128)(2,1)} %bitcast.7) | data formatting | bytes 1048576
  (9 shorter events, 0.1 us)

commit v2 on v1

--- a/solution.py
+++ b/solution.py
@@ -1,4 +1,5 @@
 import functools
+import math
 
 import jax
 import jax.numpy as jnp
@@ -23,8 +24,8 @@
 
 
 def layer(
-    near, far, slots,
-    tokens, gain, ids, scores, code_near, code_far, slot_near, slot_far, w_gate, w_up, w_down,
+    near, far, slots, experts,
+    tokens, gain, ids, scores, table, w_gate, w_up, w_down,
     out,
     gate_buf, up_buf, down_buf, normed, hits_near, hits_far, hidden, mixed,
     send_n, send_f, recv_n, recv_f, done_n, done_f, back_n, back_f,
@@ -38,8 +39,8 @@
     mine = me % half
     side = me // half
     micros, rows, width = tokens.shape
-    top = ids.shape[2]
-    experts = STRIDE
+    top = ids.shape[1]
+    rows_n, rows_f = half * near, half * far * micros
 
     loads = []
     for slot in range(slots):
@@ -66,39 +67,40 @@
     def _():
         pl.semaphore_signal(barrier, inc=1, device_id=(section + 1, me), device_id_type=MESH)
 
-    lane = lax.broadcasted_iota(jnp.int32, (rows, 128), 1)
-    lower = (
+    kinds = round_up(experts, 16)
+    kind = lax.broadcasted_iota(jnp.int32, (kinds, rows), 0)
+    earlier = (
         lax.broadcasted_iota(jnp.int32, (rows, rows), 0)
-        > lax.broadcasted_iota(jnp.int32, (rows, rows), 1)
+        < lax.broadcasted_iota(jnp.int32, (rows, rows), 1)
     ).astype(jnp.bfloat16)
+    code_near, code_far = table[:rows_n, 0:1], table[rows_n:, 0:1]
     mixing = []
     for micro in range(micros):
         values = tokens[micro].astype(jnp.float32)
         scale = lax.rsqrt(jnp.mean(values * values, axis=-1, keepdims=True) + EPSILON)
         normed[micro] = (values * scale * gain[...]).astype(jnp.bfloat16)
-        ones = [(ids[micro][:, k : k + 1] == lane).astype(jnp.float32) for k in range(top)]
+        ones = [(ids[micro, k : k + 1, :] == kind).astype(jnp.float32) for k in range(top)]
         both = functools.reduce(jnp.add, ones)
-        before = jnp.dot(lower, both.astype(jnp.bfloat16), preferred_element_type=jnp.float32)
-        chosen = scores[micro]
-        probs = chosen / jnp.sum(chosen, axis=1, keepdims=True)
+        before = jnp.dot(both.astype(jnp.bfloat16), earlier, preferred_element_type=jnp.float32)
+        chosen = [scores[micro, k : k + 1, :] for k in range(top)]
+        whole = functools.reduce(jnp.add, chosen)
         take_n = take_f = mix_n = mix_f = 0.0
         for k in range(top):
-            rank = jnp.sum(before * ones[k], axis=1, keepdims=True).astype(jnp.int32)
-            code = ids[micro][:, k : k + 1] * STRIDE + rank
-            in_n = (code == code_near[...]).astype(jnp.float32)
-            in_f = (code + micro * MARK == code_far[...]).astype(jnp.float32)
+            rank = jnp.sum(before * ones[k], axis=0, keepdims=True).astype(jnp.int32)
+            code = ids[micro, k : k + 1, :] * STRIDE + rank
+            prob = chosen[k] / whole
+            in_n = (code == code_near).astype(jnp.float32)
+            in_f = (code + micro * MARK == code_far).astype(jnp.float32)
             take_n = take_n + in_n
             take_f = take_f + in_f
-            mix_n = mix_n + in_n * probs[:, k : k + 1]
-            mix_f = mix_f + in_f * probs[:, k : k + 1]
+            mix_n = mix_n + in_n * prob
+            mix_f = mix_f + in_f * prob
         hits_near[micro] = take_n.astype(jnp.bfloat16)
         hits_far[micro] = take_f.astype(jnp.bfloat16)
         mixing.append((mix_n, mix_f))
 
     def gather(hits, source):
-        return lax.dot_general(
-            hits, source, (((0,), (0,)), ((), ())), preferred_element_type=jnp.float32
-        )
+        return jnp.dot(hits, source, preferred_element_type=jnp.float32)
 
     send_f[...] = (
         sum(gather(hits_far[micro], normed[micro]) for micro in range(micros))
@@ -182,8 +184,6 @@
 
         lax.fori_loop(0, width // wide, down_body, 0)
 
-    rows_n, rows_f = half * near, half * far * micros
-
     each(0, lambda step: far_copy(step, send_f, recv_f, to_f, from_f).wait_recv())
     each(1, lambda step: near_copy(0, step, send_n, recv_n, to_n, from_n).wait_recv())
     for copy in loads:
@@ -198,7 +198,7 @@
         lambda: jnp.concatenate(
             [recv_f[...].reshape(rows_f, width), recv_n[0].reshape(rows_n, width)], axis=0
         ),
-        jnp.concatenate([slot_far[...], slot_near[...]], axis=0),
+        jnp.concatenate([table[rows_n:, 1:2], table[:rows_n, 1:2]], axis=0),
         store_first,
     )
     each(0, lambda step: far_copy(step, done_f, back_f, ret_to_f, ret_from_f).start())
@@ -212,7 +212,7 @@
             done_n[micro, :, :, cols] = value.reshape(half, near, value.shape[1])
 
         experts_of(
-            rows_n, lambda: recv_n[micro].reshape(rows_n, width), slot_near[...], store_next
+            rows_n, lambda: recv_n[micro].reshape(rows_n, width), table[:rows_n, 1:2], store_next
         )
         each(1, lambda step: near_copy(micro, step, done_n, back_n, ret_to_n, ret_from_n).start())
         back_n[micro, mine] = done_n[micro, mine]
@@ -220,9 +220,10 @@
     def weighed(mix, values):
         high = mix.astype(jnp.bfloat16)
         low = (mix - high.astype(jnp.float32)).astype(jnp.bfloat16)
-        return jnp.dot(high, values, preferred_element_type=jnp.float32) + jnp.dot(
-            low, values, preferred_element_type=jnp.float32
-        )
+        rule = (((0,), (0,)), ((), ()))
+        return lax.dot_general(
+            high, values, rule, preferred_element_type=jnp.float32
+        ) + lax.dot_general(low, values, rule, preferred_element_type=jnp.float32)
 
     def relay(micro, by):
         return pltpu.make_async_remote_copy(
@@ -268,47 +269,152 @@
             relay(micro, by).wait_recv()
 
 
-def places(placement, devices, slot_cap, near, far):
+def plain_table(placement, devices, slot_cap, near, far, micros):
+    half = devices // 2
+    side = lax.axis_index("expert") // half
     slots = placement.shape[0]
+    per = slots // devices
     slot_range = jnp.arange(slots, dtype=jnp.int32)
     same = placement[:, None] == placement[None, :]
     copies = jnp.sum(same, axis=1, dtype=jnp.int32)
     replica = jnp.sum(same & (slot_range[None, :] < slot_range[:, None]), axis=1, dtype=jnp.int32)
     index = jnp.arange(slot_cap, dtype=jnp.int32)
     code = placement[:, None] * STRIDE + index[None, :] * copies[:, None] + replica[:, None]
-    per = slots // devices
     code = code.reshape(devices, per * slot_cap)
     owner = jnp.broadcast_to(jnp.arange(per, dtype=jnp.int32)[:, None], (per, slot_cap)).reshape(-1)
     fill_n, fill_f = near - per * slot_cap, far - per * slot_cap
     code_n = jnp.pad(code, ((0, 0), (0, fill_n)), constant_values=-1)
     code_f = jnp.pad(code, ((0, 0), (0, fill_f)), constant_values=-1)
-    return code_n, code_f, jnp.pad(owner, (0, fill_n)), jnp.pad(owner, (0, fill_f))
-
-
-def body(tokens, norm_gain, expert_ids, route_scores, placement, w_gate, w_up, w_down):
+    code_n = lax.dynamic_slice_in_dim(code_n, side * half, half, 0).reshape(-1)
+    code_f = lax.dynamic_slice_in_dim(code_f, (1 - side) * half, half, 0)[:, None, :]
+    marks = jnp.arange(micros, dtype=jnp.int32)[None, :, None] * MARK
+    code_f = jnp.where(code_f >= 0, code_f + marks, -1).reshape(-1)
+    slot_n = jnp.tile(jnp.pad(owner, (0, fill_n)), half)
+    slot_f = jnp.tile(jnp.pad(owner, (0, fill_f)), half * micros)
+    columns = jnp.stack(
+        [jnp.concatenate([code_n, code_f]), jnp.concatenate([slot_n, slot_f])], axis=1
+    )
+    return jnp.pad(columns, ((0, 0), (0, 126)))
+
+
+def plan(near, far, micros, experts, most, held, table, fits):
+    devices, per = held.shape
+    half = devices // 2
+    me = lax.axis_index("expert")
+    side = me // half
+    f32 = jnp.float32
+    shape = (devices, 128)
+    lane = lax.broadcasted_iota(jnp.int32, shape, 1)
+    device = lax.broadcasted_iota(jnp.int32, shape, 0)
+    from_half = lane // 64
+    attempt = lane % 64
+    strides = [a for a in range(1, experts) if math.gcd(a, experts) == 1][: max(1, 64 // experts)]
+    turn = attempt // experts
+    stride = jnp.full(shape, strides[0], jnp.int32)
+    for i, a in enumerate(strides):
+        stride = jnp.where(turn == i, a, stride)
+    weight = jnp.where(device // half == from_half, far, near)
+    limit = near * far
+    owned = [held[:, j : j + 1] for j in range(per)]
+    order, holds = [], []
+    now = attempt % experts
+    for _ in range(experts):
+        order.append(now)
+        holds.append(functools.reduce(jnp.logical_or, [o == now for o in owned]))
+        now = now + stride
+        now = jnp.where(now >= experts, now - experts, now)
+    load = jnp.zeros(shape, jnp.int32)
+    given = [jnp.zeros(shape, jnp.int32)] * experts
+    chunks = [most - most // 2, most // 2]
+    for _ in range(2):
+        for step in range(experts):
+            load = load - given[step]
+            share = jnp.zeros(shape, jnp.int32)
+            for chunk in chunks:
+                key = jnp.where(holds[step], (load + chunk) * weight * devices + device, 1 << 30)
+                best = jnp.min(key, axis=0, keepdims=True)
+                more = jnp.where(key == best, chunk, 0)
+                load = load + more
+                share = share + more
+            given[step] = share
+    worst = jnp.max(load * weight, axis=0, keepdims=True)
+    lane_row = lax.broadcasted_iota(jnp.int32, (1, 128), 1)
+    rating = worst * 128 + lane_row
+    half_row = lane_row // 64
+    ratings = [
+        jnp.min(jnp.where(half_row == h, rating, 1 << 30), axis=1, keepdims=True) for h in range(2)
+    ]
+    fits[...] = jnp.broadcast_to(
+        (jnp.maximum(ratings[0], ratings[1]) < (limit + 1) * 128).astype(jnp.int32), fits.shape
+    )
+
+    def columns(from_side, length, width, period, to_device):
+        rating_there = jnp.where(from_side == 0, ratings[0], ratings[1])
+        picked = (rating == rating_there) & (half_row == from_side)
+        amount = jnp.zeros(shape, f32)
+        kinds = jnp.zeros((1, 128), f32)
+        for step in range(experts):
+            mine = jnp.sum(jnp.where(picked, given[step], 0).astype(f32), axis=1, keepdims=True)
+            kind = jnp.sum(
+                jnp.where(picked, order[step][:1], 0).astype(f32), axis=1, keepdims=True
+            )
+            amount = amount + jnp.where(lane == step, mine, 0.0)
+            kinds = kinds + jnp.where(lane_row == step, kind, 0.0)
+        first = jnp.dot(
+            (
+                lax.broadcasted_iota(jnp.int32, (devices, devices), 1)
+                < lax.broadcasted_iota(jnp.int32, (devices, devices), 0)
+            ).astype(f32),
+            amount,
+            preferred_element_type=f32,
+        )
+        ahead = jnp.dot(
+            amount,
+            (
+                lax.broadcasted_iota(jnp.int32, (128, 128), 0)
+                < lax.broadcasted_iota(jnp.int32, (128, 128), 1)
+            ).astype(f32),
+            preferred_element_type=f32,
+        )
+        local = jnp.zeros(shape, f32)
+        for j in reversed(range(per)):
+            local = jnp.where(owned[j].astype(f32) == kinds, float(j), local)
+        row = lax.broadcasted_iota(jnp.int32, (length, 1), 0)
+        place = (row % period).astype(f32)
+        target = (
+            lax.broadcasted_iota(jnp.int32, (length, devices), 1) == to_device(row // width)
+        ).astype(f32)
+
+        def spread(values):
+            return jnp.dot(target, values, preferred_element_type=f32)
+
+        start = spread(ahead)
+        inside = ((place >= start) & (place < start + spread(amount))).astype(f32)
+        numbers = kinds * STRIDE + place - start + spread(first)
+        code = jnp.sum(inside * (numbers + 1.0), axis=1, keepdims=True).astype(jnp.int32) - 1
+        slot = jnp.sum(inside * spread(local), axis=1, keepdims=True).astype(jnp.int32)
+        return code, slot, row
+
+    rows_n, rows_f = half * near, half * far * micros
+    code_n, _, _ = columns(side, rows_n, near, near, lambda block: side * half + block)
+    code_f, _, row_f = columns(
+        side, rows_f, far * micros, far, lambda block: (1 - side) * half + block
+    )
+    code_f = jnp.where(code_f >= 0, code_f + row_f % (far * micros) // far * MARK, -1)
+    _, slot_n, _ = columns(side, rows_n, near, near, lambda block: me + 0 * block)
+    _, slot_f, _ = columns(1 - side, rows_f, far * micros, far, lambda block: me + 0 * block)
+    column = lax.broadcasted_iota(jnp.int32, (rows_n, 128), 1)
+    table[:rows_n] = jnp.where(column == 0, code_n, slot_n)
+    column = lax.broadcasted_iota(jnp.int32, (rows_f, 128), 1)
+    table[rows_n:] = jnp.where(column == 0, code_f, slot_f)
+
+
+def routed(call, near, far, experts, table, tokens, gain, ids, scores, w_gate, w_up, w_down):
     devices = lax.axis_size("expert")
     half = devices // 2
-    side = lax.axis_index("expert") // half
     slots = w_gate.shape[0]
     ff = w_gate.shape[2]
-    micros, _, rows, width = tokens.shape
-    top = expert_ids.shape[3]
-    experts = placement.shape[0] * 3 // 8
-    most = (rows * top + experts - 1) // experts
-    slot_cap = (most + 1) // 2
-    near = round_up(slots * slot_cap, 16)
-    far = round_up(slots * slot_cap, 8)
-    code_n, code_f, owner_n, owner_f = places(placement, devices, slot_cap, near, far)
-
-    code_near = lax.dynamic_slice_in_dim(code_n, side * half, half, 0).reshape(1, half * near)
-    code_there = lax.dynamic_slice_in_dim(code_f, (1 - side) * half, half, 0)
-    marks = jnp.arange(micros, dtype=jnp.int32) * MARK
-    code_far = jnp.where(
-        code_there[:, None, :] >= 0, code_there[:, None, :] + marks[None, :, None], -1
-    ).reshape(1, half * micros * far)
-    slot_near = jnp.broadcast_to(owner_n[None, :], (half, near)).reshape(half * near, 1)
-    slot_far = jnp.broadcast_to(owner_f[None, None, :], (half, micros, far)).reshape(-1, 1)
-
+    micros, rows, width = tokens.shape
     rows_n, rows_f = half * near, half * micros * far
     vmem = pl.BlockSpec(memory_space=pltpu.VMEM)
     block = split_columns(ff)
@@ -316,18 +422,18 @@
     f_shape = (half, micros * far, width)
     bf16 = jnp.bfloat16
     dma = pltpu.SemaphoreType.DMA
-    result = pl.pallas_call(
-        functools.partial(layer, near, far, slots),
+    return pl.pallas_call(
+        functools.partial(layer, near, far, slots, experts),
         out_shape=jax.ShapeDtypeStruct((micros, rows, width), bf16),
-        in_specs=[vmem] * 8 + [pl.BlockSpec(memory_space=pl.ANY)] * 3,
+        in_specs=[vmem] * 5 + [pl.BlockSpec(memory_space=pl.ANY)] * 3,
         out_specs=vmem,
         scratch_shapes=[
             pltpu.VMEM(w_gate.shape, bf16),
             pltpu.VMEM(w_up.shape, bf16),
             pltpu.VMEM(w_down.shape, bf16),
             pltpu.VMEM((micros, rows, width), bf16),
-            pltpu.VMEM((micros, rows, rows_n), bf16),
-            pltpu.VMEM((micros, rows, rows_f), bf16),
+            pltpu.VMEM((micros, rows_n, rows), bf16),
+            pltpu.VMEM((micros, rows_f, rows), bf16),
             pltpu.VMEM((slots * (ff // block), rows_n + rows_f, block), bf16),
             pltpu.VMEM((micros, rows, width), bf16),
             pltpu.VMEM(n_shape, bf16),
@@ -351,11 +457,53 @@
             dma((micros,)),
         ],
         compiler_params=pltpu.CompilerParams(
-            collective_id=0, has_side_effects=True, vmem_limit_bytes=62 << 20
+            collective_id=call, has_side_effects=True, vmem_limit_bytes=62 << 20
         ),
-    )(
-        tokens[:, 0], norm_gain[None, :], expert_ids[:, 0], route_scores[:, 0],
-        code_near, code_far, slot_near, slot_far, w_gate, w_up, w_down,
+    )(tokens, gain, ids, scores, table, w_gate, w_up, w_down)
+
+
+def body(tokens, norm_gain, expert_ids, route_scores, placement, w_gate, w_up, w_down):
+    devices = lax.axis_size("expert")
+    half = devices // 2
+    slots = w_gate.shape[0]
+    micros, _, rows, width = tokens.shape
+    top = expert_ids.shape[3]
+    experts = placement.shape[0] * 3 // 8
+    most = (rows * top + experts - 1) // experts
+    slot_cap = (most + 1) // 2
+    arrays = (
+        tokens[:, 0],
+        norm_gain[None, :],
+        jnp.swapaxes(expert_ids[:, 0], 1, 2),
+        jnp.swapaxes(route_scores[:, 0], 1, 2),
+        w_gate,
+        w_up,
+        w_down,
+    )
+
+    def plain():
+        near = round_up(slots * slot_cap, 16)
+        far = round_up(slots * slot_cap, 8)
+        table = plain_table(placement, devices, slot_cap, near, far, micros)
+        return routed(0, near, far, experts, table, *arrays)
+
+    if devices != 8 or slots < 2:
+        return plain()[:, None]
+    near = round_up(rows * top // half, 16)
+    far = near * 3 // 8
+    rows_all = half * (near + far * micros)
+    vmem = pl.BlockSpec(memory_space=pltpu.VMEM)
+    table, fits = pl.pallas_call(
+        functools.partial(plan, near, far, micros, experts, most),
+        out_shape=(
+            jax.ShapeDtypeStruct((rows_all, 128), jnp.int32),
+            jax.ShapeDtypeStruct((8, 128), jnp.int32),
+        ),
+        in_specs=[vmem],
+        out_specs=(vmem, vmem),
+    )(placement.reshape(devices, slots))
+    result = lax.cond(
+        fits[0, 0] > 0, lambda: routed(1, near, far, experts, table, *arrays), plain
     )
     return result[:, None]
 

time: 107 us -> 70.4 us (0.66)
  the two profiles are of different devices: /device:TPU:1 before, /device:TPU:13 now
where the time goes in v2:
time: 70.4 us; the launch traced here: 70.2 us
  Pallas kernels  66.2 us (94%)
  local copies, waits for them, and re-layouts  3.31 us (5%)
    pallas_call x1, Pallas kernels, routed(): pl.pallas_call(functools.partial(layer, near, far, slots, experts), out_s...  64 us
    pallas_call x1, Pallas kernels, body(): pl.pallas_call(functools.partial(plan, near, far, micros, experts, most),...  2.16 us

profile of v2, /device:TPU:13, one launch (start us, length us, event | category | flops | bytes accessed | tf_op | source)
XLA Modules:
  0.0 70.2 jit_solution(15343512602219262097)
XLA Ops:
  0.0 1.3 %reshape.50.held = s32[8,4]{1,0:T(8,128)} reshape(s32[32]{0:T(128)} %param.14) | data formatting | bytes 256 | tf_op jit(solution)/shard_map/reshape | solution.py:504
  1.3 2.2 %shard_map.84 = (s32[224,128]{1,0:T(8,128)S(1)}, s32[8,128]{1,0:T(8,128)}) custom-call(s32[8,4]{1,0:T(8,128)} %reshape.50.held), custom_call_target="tpu_custom_call" | custom-call | tf_op jit(solution)/shard_map/pallas_call | solution.py:496
  3.5 1.2 %slice.3 = s32[1,1]{1,0:T(1,128)} slice(s32[8,128]{1,0:T(8,128)} %get-tuple-element.59), slice={[0:1], [0:1]} | slice | bytes 8 | tf_op jit(solution)/shard_map/slice | solution.py:506
  5.3 64.1 %conditional.1 = (bf16[2,1,64,2048]{3,2,1,0:T(8,128)(2,1)S(1)}) conditional(s32[]{:T(128)} %bitcast.6, (s32[32]{0:T(128)}, bf16[2,64,2048]{2,1,0:T(8,128)(2,1)}, f32[1,2048]{1,0:T(1,128)}, s32[2,2,64]{2,1,0:T(2,128)}, f32[2,2,64]{2,1,0:T(2,128)}, /*index=5*/bf16[4,2048,768]{2,1,0:T(8,128)(2,1)}, bf16[4,2048,768]{2,1,0:T(8,128)(2,1)}, ...), branch_computations={%region_0.3_spmd, %region_3.4_spmd} | conditional | flops 9500 | bytes 209882 | solution.py:505
  5.3 64.0 %branch_1_fun.1 = bf16[2,64,2048]{2,1,0:T(8,128)(2,1)S(1)} custom-call(bf16[2,64,2048]{2,1,0:T(8,128)(2,1)} %get-tuple-element.49.tokens, f32[1,2048]{1,0:T(1,128)} %get-tuple-element.50.gain, s32[2,2,64]{2,1,0:T(2,128)} %get-tuple-element.51.ids, f32[2,2,64]{2,1,0:T(2,128)} %get-tuple-element.52.scores, s32[224,128]{1,0:T(8,128)S(1)} %get-tuple-element.53.table, ...), custom_call_target="tpu_custom_call" | custom-call | tf_op jit(solution)/shard_map/cond/branch_1_fun/pallas_call | solution.py:425
  69.4 0.8 %copy.24 = bf16[2,1,64,2048]{3,2,1,0:T(8,128)(2,1)} copy(bf16[2,1,64,2048]{3,2,1,0:T(8,128)(2,1)S(1)} %get-tuple-element.62) | data formatting | bytes 1048576

commit v3 on v2

--- a/solution.py
+++ b/solution.py
@@ -13,6 +13,7 @@
 MARK = 1 << 20
 MESH = pl.DeviceIdType.MESH
 COLUMNS = 256
+PIECES = 4
 
 
 def round_up(value, to):
@@ -27,7 +28,7 @@
     near, far, slots, experts,
     tokens, gain, ids, scores, table, w_gate, w_up, w_down,
     out,
-    gate_buf, up_buf, down_buf, normed, hits_near, hits_far, hidden, mixed,
+    gate_buf, up_buf, down_buf, normed, hits_near, hits_far, hidden, mixed, partial,
     send_n, send_f, recv_n, recv_f, done_n, done_f, back_n, back_f,
     weight_sem, to_n, from_n, to_f, from_f, ret_to_n, ret_from_n, ret_to_f, ret_from_f, relay_to, relay_from,
 ):
@@ -42,12 +43,12 @@
     top = ids.shape[1]
     rows_n, rows_f = half * near, half * far * micros
 
-    loads = []
-    for slot in range(slots):
-        for kind, (src, dst) in enumerate(((w_gate, gate_buf), (w_up, up_buf), (w_down, down_buf))):
-            copy = pltpu.make_async_copy(src.at[slot], dst.at[slot], weight_sem.at[kind, slot])
-            copy.start()
-            loads.append(copy)
+    for kind, (src, dst) in enumerate(((w_gate, gate_buf), (w_up, up_buf), (w_down, down_buf))):
+        for slot in range(slots):
+            if kind != 1:
+                pltpu.make_async_copy(src.at[slot], dst.at[slot], weight_sem.at[kind, slot]).start()
+            if kind == 0:
+                pltpu.make_async_copy(w_up.at[slot], up_buf.at[slot], weight_sem.at[1, slot]).start()
 
     barrier = pltpu.get_barrier_semaphore()
 
@@ -102,12 +103,6 @@
     def gather(hits, source):
         return jnp.dot(hits, source, preferred_element_type=jnp.float32)
 
-    send_f[...] = (
-        sum(gather(hits_far[micro], normed[micro]) for micro in range(micros))
-        .astype(jnp.bfloat16)
-        .reshape(send_f.shape)
-    )
-
     greeted = (
         peers - 1 + (section > 0).astype(jnp.int32) + (section < sections - 1).astype(jnp.int32)
     )
@@ -142,21 +137,46 @@
 
         lax.fori_loop(first, half, step_body, 0)
 
-    each(0, lambda step: far_copy(step, send_f, recv_f, to_f, from_f).start())
     for micro in range(micros):
         send_n[micro] = (
             gather(hits_near[micro], normed[micro]).astype(jnp.bfloat16).reshape(send_n.shape[1:])
         )
         each(1, lambda step: near_copy(micro, step, send_n, recv_n, to_n, from_n).start())
         recv_n[micro, mine] = send_n[micro, mine]
-
-    def experts_of(count, inputs, owner, store):
+        if micro == 0:
+            send_f[...] = (
+                sum(gather(hits_far[micro], normed[micro]) for micro in range(micros))
+                .astype(jnp.bfloat16)
+                .reshape(send_f.shape)
+            )
+            each(0, lambda step: far_copy(step, send_f, recv_f, to_f, from_f).start())
+
+    def load(kind, slot):
+        src, dst = ((w_gate, gate_buf), (w_up, up_buf), (w_down, down_buf))[kind]
+        return pltpu.make_async_copy(src.at[slot], dst.at[slot], weight_sem.at[kind, slot])
+
+    def loaded(kinds):
+        def loaded_body(slot, carry):
+            for kind in kinds:
+                load(kind, slot).wait()
+            return carry
+
+        lax.fori_loop(0, slots, loaded_body, 0)
+
+    def experts_of(count, inputs, owner, store, fresh=False, sent=None):
         ff = gate_buf.shape[2]
         block = split_columns(ff)
         per = ff // block
 
         def up_body(step, carry):
             slot = step // per
+            if fresh:
+
+                @pl.when(step % per == 0)
+                def _():
+                    load(0, slot).wait()
+                    load(1, slot).wait()
+
             cols = pl.ds(pl.multiple_of((step % per) * block, block), block)
             x = inputs()
             gate = jnp.dot(x, gate_buf[slot, :, cols], preferred_element_type=jnp.float32)
@@ -167,7 +187,10 @@
             return carry
 
         lax.fori_loop(0, slots * per, up_body, 0)
+        if fresh:
+            loaded((2,))
         wide = split_columns(width)
+        group = width // wide // PIECES
 
         def down_body(step, carry):
             cols = pl.ds(pl.multiple_of(step * wide, wide), wide)
@@ -180,42 +203,57 @@
                         preferred_element_type=jnp.float32,
                     )
             store(cols, total.astype(jnp.bfloat16))
+            if sent is not None:
+
+                @pl.when(step % group == group - 1)
+                def _():
+                    sent(step // group)
+
             return carry
 
         lax.fori_loop(0, width // wide, down_body, 0)
 
-    each(0, lambda step: far_copy(step, send_f, recv_f, to_f, from_f).wait_recv())
-    each(1, lambda step: near_copy(0, step, send_n, recv_n, to_n, from_n).wait_recv())
-    for copy in loads:
-        copy.wait()
-
-    def store_first(cols, value):
-        done_f[:, :, cols] = value[:rows_f].reshape(half, far * micros, value.shape[1])
-        done_n[0, :, :, cols] = value[rows_f:].reshape(half, near, value.shape[1])
-
-    experts_of(
-        rows_f + rows_n,
-        lambda: jnp.concatenate(
-            [recv_f[...].reshape(rows_f, width), recv_n[0].reshape(rows_n, width)], axis=0
-        ),
-        jnp.concatenate([table[rows_n:, 1:2], table[:rows_n, 1:2]], axis=0),
-        store_first,
-    )
-    each(0, lambda step: far_copy(step, done_f, back_f, ret_to_f, ret_from_f).start())
-    each(1, lambda step: near_copy(0, step, done_n, back_n, ret_to_n, ret_from_n).start())
-    back_n[0, mine] = done_n[0, mine]
-
-    for micro in range(1, micros):
+    for micro in range(micros):
         each(1, lambda step: near_copy(micro, step, send_n, recv_n, to_n, from_n).wait_recv())
 
-        def store_next(cols, value):
+        def store_near(cols, value):
             done_n[micro, :, :, cols] = value.reshape(half, near, value.shape[1])
 
         experts_of(
-            rows_n, lambda: recv_n[micro].reshape(rows_n, width), table[:rows_n, 1:2], store_next
+            rows_n,
+            lambda: recv_n[micro].reshape(rows_n, width),
+            table[:rows_n, 1:2],
+            store_near,
+            fresh=micro == 0,
         )
         each(1, lambda step: near_copy(micro, step, done_n, back_n, ret_to_n, ret_from_n).start())
         back_n[micro, mine] = done_n[micro, mine]
+
+    piece = width // PIECES
+
+    def far_return(step, part):
+        there = (mine + step) % half
+        cols = pl.ds(pl.multiple_of(part * piece, piece), piece)
+        return pltpu.make_async_remote_copy(
+            src_ref=done_f.at[there, :, cols],
+            dst_ref=back_f.at[mine, :, cols],
+            send_sem=ret_to_f.at[part, step],
+            recv_sem=ret_from_f.at[part, step],
+            device_id=(section, (1 - side) * half + there),
+            device_id_type=MESH,
+        )
+
+    def store_far(cols, value):
+        done_f[:, :, cols] = value.reshape(half, far * micros, value.shape[1])
+
+    each(0, lambda step: far_copy(step, send_f, recv_f, to_f, from_f).wait_recv())
+    experts_of(
+        rows_f,
+        lambda: recv_f[...].reshape(rows_f, width),
+        table[rows_n:, 1:2],
+        store_far,
+        sent=lambda part: each(0, lambda step: far_return(step, part).start()),
+    )
 
     def weighed(mix, values):
         high = mix.astype(jnp.bfloat16)
@@ -225,48 +263,57 @@
             high, values, rule, preferred_element_type=jnp.float32
         ) + lax.dot_general(low, values, rule, preferred_element_type=jnp.float32)
 
-    def relay(micro, by):
+    def relay(micro, by, part):
+        cols = pl.ds(part * piece, piece)
         return pltpu.make_async_remote_copy(
-            src_ref=mixed.at[micro],
-            dst_ref=out.at[micro],
-            send_sem=relay_to.at[micro],
-            recv_sem=relay_from.at[micro],
+            src_ref=mixed.at[micro, :, cols],
+            dst_ref=out.at[micro, :, cols],
+            send_sem=relay_to.at[micro, part],
+            recv_sem=relay_from.at[micro, part],
             device_id=(section + by, me),
             device_id_type=MESH,
         )
 
-    each(0, lambda step: far_copy(step, done_f, back_f, ret_to_f, ret_from_f).wait_recv())
     sends = ((0, 1, section < sections - 1, section > 0), (1, -1, section > 0, section < sections - 1))
     for micro, by, gives, gets in sends:
         each(1, lambda step: near_copy(micro, step, done_n, back_n, ret_to_n, ret_from_n).wait_recv())
-        mix_n, mix_f = mixing[micro]
-        total = tokens[micro].astype(jnp.float32)
-        total = total + weighed(mix_f, back_f[...].reshape(rows_f, width))
-        total = total + weighed(mix_n, back_n[micro].reshape(rows_n, width))
-        mixed[micro] = total.astype(jnp.bfloat16)
-
-        @pl.when(gives)
-        def _():
-            relay(micro, by).start()
+        partial[micro] = tokens[micro].astype(jnp.float32) + weighed(
+            mixing[micro][0], back_n[micro].reshape(rows_n, width)
+        )
 
         @pl.when(jnp.logical_not(gets))
         def _():
             out[micro] = jnp.zeros(out.shape[1:], out.dtype)
 
+    for part in range(PIECES):
+        cols = pl.ds(part * piece, piece)
+        each(0, lambda step: far_return(step, part).wait_recv())
+        for micro, by, gives, gets in sends:
+            total = partial[micro, :, cols] + weighed(
+                mixing[micro][1], back_f[:, :, cols].reshape(rows_f, piece)
+            )
+            mixed[micro, :, cols] = total.astype(jnp.bfloat16)
+
+            @pl.when(gives)
+            def _():
+                relay(micro, by, part).start()
+
     each(0, lambda step: far_copy(step, send_f, recv_f, to_f, from_f).wait_send())
-    each(0, lambda step: far_copy(step, done_f, back_f, ret_to_f, ret_from_f).wait_send())
+    for part in range(PIECES):
+        each(0, lambda step: far_return(step, part).wait_send())
     for micro in range(micros):
         each(1, lambda step: near_copy(micro, step, send_n, recv_n, to_n, from_n).wait_send())
         each(1, lambda step: near_copy(micro, step, done_n, back_n, ret_to_n, ret_from_n).wait_send())
     for micro, by, gives, gets in sends:
-
-        @pl.when(gives)
-        def _():
-            relay(micro, by).wait_send()
-
-        @pl.when(gets)
-        def _():
-            relay(micro, by).wait_recv()
+        for part in range(PIECES):
+
+            @pl.when(gives)
+            def _():
+                relay(micro, by, part).wait_send()
+
+            @pl.when(gets)
+            def _():
+                relay(micro, by, part).wait_recv()
 
 
 def plain_table(placement, devices, slot_cap, near, far, micros):
@@ -297,8 +344,8 @@
     return jnp.pad(columns, ((0, 0), (0, 126)))
 
 
-def plan(near, far, micros, experts, most, held, table, fits):
-    devices, per = held.shape
+def plan(devices, near, far, micros, experts, most, held, table, fits):
+    per = held.shape[1] // devices
     half = devices // 2
     me = lax.axis_index("expert")
     side = me // half
@@ -315,7 +362,13 @@
         stride = jnp.where(turn == i, a, stride)
     weight = jnp.where(device // half == from_half, far, near)
     limit = near * far
-    owned = [held[:, j : j + 1] for j in range(per)]
+    spot = lax.broadcasted_iota(jnp.int32, (devices, held.shape[1]), 1)
+    first_spot = lax.broadcasted_iota(jnp.int32, (devices, held.shape[1]), 0) * per
+    owned = [
+        jnp.sum(jnp.where(spot == first_spot + j, held[...], 0).astype(f32), axis=1, keepdims=True)
+        .astype(jnp.int32)
+        for j in range(per)
+    ]
     order, holds = [], []
     now = attempt % experts
     for _ in range(experts):
@@ -344,9 +397,7 @@
     ratings = [
         jnp.min(jnp.where(half_row == h, rating, 1 << 30), axis=1, keepdims=True) for h in range(2)
     ]
-    fits[...] = jnp.broadcast_to(
-        (jnp.maximum(ratings[0], ratings[1]) < (limit + 1) * 128).astype(jnp.int32), fits.shape
-    )
+    fits[0] = (jnp.max(jnp.maximum(ratings[0], ratings[1])) < (limit + 1) * 128).astype(jnp.int32)
 
     def columns(from_side, length, width, period, to_device):
         rating_there = jnp.where(from_side == 0, ratings[0], ratings[1])
@@ -434,8 +485,9 @@
             pltpu.VMEM((micros, rows, width), bf16),
             pltpu.VMEM((micros, rows_n, rows), bf16),
             pltpu.VMEM((micros, rows_f, rows), bf16),
-            pltpu.VMEM((slots * (ff // block), rows_n + rows_f, block), bf16),
+            pltpu.VMEM((slots * (ff // block), max(rows_n, rows_f), block), bf16),
             pltpu.VMEM((micros, rows, width), bf16),
+            pltpu.VMEM((micros, rows, width), jnp.float32),
             pltpu.VMEM(n_shape, bf16),
             pltpu.VMEM(f_shape, bf16),
             pltpu.VMEM(n_shape, bf16),
@@ -451,10 +503,10 @@
             dma((half,)),
             dma((micros, half)),
             dma((micros, half)),
-            dma((half,)),
-            dma((half,)),
-            dma((micros,)),
-            dma((micros,)),
+            dma((PIECES, half)),
+            dma((PIECES, half)),
+            dma((micros, PIECES)),
+            dma((micros, PIECES)),
         ],
         compiler_params=pltpu.CompilerParams(
             collective_id=call, has_side_effects=True, vmem_limit_bytes=62 << 20
@@ -494,16 +546,16 @@
     rows_all = half * (near + far * micros)
     vmem = pl.BlockSpec(memory_space=pltpu.VMEM)
     table, fits = pl.pallas_call(
-        functools.partial(plan, near, far, micros, experts, most),
+        functools.partial(plan, devices, near, far, micros, experts, most),
         out_shape=(
             jax.ShapeDtypeStruct((rows_all, 128), jnp.int32),
-            jax.ShapeDtypeStruct((8, 128), jnp.int32),
+            jax.ShapeDtypeStruct((1,), jnp.int32),
         ),
         in_specs=[vmem],
-        out_specs=(vmem, vmem),
-    )(placement.reshape(devices, slots))
+        out_specs=(vmem, pl.BlockSpec(memory_space=pltpu.SMEM)),
+    )(placement[None, :])
     result = lax.cond(
-        fits[0, 0] > 0, lambda: routed(1, near, far, experts, table, *arrays), plain
+        fits[0] > 0, lambda: routed(1, near, far, experts, table, *arrays), plain
     )
     return result[:, None]
 

time: 70.4 us -> 71.1 us (level)
  the two profiles are of different devices: /device:TPU:13 before, /device:TPU:1 now
where the time goes in v3:
time: 71.1 us; the launch traced here: 71 us
  Pallas kernels  69.5 us (98%)
  local copies, waits for them, and re-layouts  0.8 us (1%)
    pallas_call x1, Pallas kernels, routed(): pl.pallas_call(functools.partial(layer, near, far, slots, experts), out_s...  67.3 us
    pallas_call x1, Pallas kernels, body(): pl.pallas_call(functools.partial(plan, devices, near, far, micros, expert...  2.15 us

profile of v3, /device:TPU:1, one launch (start us, length us, event | category | flops | bytes accessed | tf_op | source)
XLA Modules:
  0.0 71.0 jit_solution(9696711370300661875)
XLA Ops:
  0.0 2.2 %shard_map.84 = (s32[224,128]{1,0:T(8,128)S(1)}, s32[1]{0:T(128)}) custom-call(s32[1,32]{1,0:T(1,128)} %bitcast.26), custom_call_target="tpu_custom_call" | custom-call | tf_op jit(solution)/shard_map/pallas_call | solution.py:548
  2.8 67.3 %conditional.1 = (bf16[2,1,64,2048]{3,2,1,0:T(8,128)(2,1)S(1)}) conditional(s32[]{:T(128)} %bitcast.7, (s32[32]{0:T(128)}, bf16[2,64,2048]{2,1,0:T(8,128)(2,1)}, f32[1,2048]{1,0:T(1,128)}, s32[2,2,64]{2,1,0:T(2,128)}, f32[2,2,64]{2,1,0:T(2,128)}, /*index=5*/bf16[4,2048,768]{2,1,0:T(8,128)(2,1)}, bf16[4,2048,768]{2,1,0:T(8,128)(2,1)}, ...), branch_computations={%region_0.3_spmd, %region_3.4_spmd} | conditional | flops 9500 | bytes 209882 | solution.py:557
  2.8 67.3 %branch_1_fun.1 = bf16[2,64,2048]{2,1,0:T(8,128)(2,1)S(1)} custom-call(bf16[2,64,2048]{2,1,0:T(8,128)(2,1)} %get-tuple-element.49.tokens, f32[1,2048]{1,0:T(1,128)} %get-tuple-element.50.gain, s32[2,2,64]{2,1,0:T(2,128)} %get-tuple-element.51.ids, f32[2,2,64]{2,1,0:T(2,128)} %get-tuple-element.52.scores, s32[224,128]{1,0:T(8,128)S(1)} %get-tuple-element.53.table, ...), custom_call_target="tpu_custom_call" | custom-call | tf_op jit(solution)/shard_map/cond/branch_1_fun/pallas_call | solution.py:476
  70.2 0.8 %copy.24 = bf16[2,1,64,2048]{3,2,1,0:T(8,128)(2,1)} copy(bf16[2,1,64,2048]{3,2,1,0:T(8,128)(2,1)S(1)} %get-tuple-element.62) | data formatting | bytes 1048576

commit v4 on v3

--- a/solution.py
+++ b/solution.py
@@ -12,23 +12,18 @@
 STRIDE = 1024
 MARK = 1 << 20
 MESH = pl.DeviceIdType.MESH
-COLUMNS = 256
 PIECES = 4
 
 
 def round_up(value, to):
     return (value + to - 1) // to * to
-
-
-def split_columns(width):
-    return COLUMNS if width % COLUMNS == 0 else width
 
 
 def layer(
     near, far, slots, experts,
     tokens, gain, ids, scores, table, w_gate, w_up, w_down,
     out,
-    gate_buf, up_buf, down_buf, normed, hits_near, hits_far, hidden, mixed, partial,
+    gate_buf, up_buf, down_buf, normed, hits_near, hits_far, hidden, mixed, partial, far_rows,
     send_n, send_f, recv_n, recv_f, done_n, done_f, back_n, back_f,
     weight_sem, to_n, from_n, to_f, from_f, ret_to_n, ret_from_n, ret_to_f, ret_from_f, relay_to, relay_from,
 ):
@@ -143,13 +138,12 @@
         )
         each(1, lambda step: near_copy(micro, step, send_n, recv_n, to_n, from_n).start())
         recv_n[micro, mine] = send_n[micro, mine]
-        if micro == 0:
-            send_f[...] = (
-                sum(gather(hits_far[micro], normed[micro]) for micro in range(micros))
-                .astype(jnp.bfloat16)
-                .reshape(send_f.shape)
-            )
-            each(0, lambda step: far_copy(step, send_f, recv_f, to_f, from_f).start())
+    send_f[...] = (
+        sum(gather(hits_far[micro], normed[micro]) for micro in range(micros))
+        .astype(jnp.bfloat16)
+        .reshape(send_f.shape)
+    )
+    each(0, lambda step: far_copy(step, send_f, recv_f, to_f, from_f).start())
 
     def load(kind, slot):
         src, dst = ((w_gate, gate_buf), (w_up, up_buf), (w_down, down_buf))[kind]
@@ -165,7 +159,7 @@
 
     def experts_of(count, inputs, owner, store, fresh=False, sent=None):
         ff = gate_buf.shape[2]
-        block = split_columns(ff)
+        block = hidden.shape[2]
         per = ff // block
 
         def up_body(step, carry):
@@ -189,8 +183,7 @@
         lax.fori_loop(0, slots * per, up_body, 0)
         if fresh:
             loaded((2,))
-        wide = split_columns(width)
-        group = width // wide // PIECES
+        wide = width // PIECES
 
         def down_body(step, carry):
             cols = pl.ds(pl.multiple_of(step * wide, wide), wide)
@@ -204,10 +197,7 @@
                     )
             store(cols, total.astype(jnp.bfloat16))
             if sent is not None:
-
-                @pl.when(step % group == group - 1)
-                def _():
-                    sent(step // group)
+                sent(step)
 
             return carry
 
@@ -216,16 +206,17 @@
     for micro in range(micros):
         each(1, lambda step: near_copy(micro, step, send_n, recv_n, to_n, from_n).wait_recv())
 
-        def store_near(cols, value):
-            done_n[micro, :, :, cols] = value.reshape(half, near, value.shape[1])
-
-        experts_of(
-            rows_n,
-            lambda: recv_n[micro].reshape(rows_n, width),
-            table[:rows_n, 1:2],
-            store_near,
-            fresh=micro == 0,
-        )
+    def store_near(cols, value):
+        done_n[:, :, :, cols] = value.reshape(micros, half, near, value.shape[1])
+
+    experts_of(
+        rows_n * micros,
+        lambda: recv_n[...].reshape(rows_n * micros, width),
+        jnp.concatenate([table[:rows_n, 1:2]] * micros, axis=0),
+        store_near,
+        fresh=True,
+    )
+    for micro in range(micros):
         each(1, lambda step: near_copy(micro, step, done_n, back_n, ret_to_n, ret_from_n).start())
         back_n[micro, mine] = done_n[micro, mine]
 
@@ -247,9 +238,10 @@
         done_f[:, :, cols] = value.reshape(half, far * micros, value.shape[1])
 
     each(0, lambda step: far_copy(step, send_f, recv_f, to_f, from_f).wait_recv())
+    far_rows[...] = recv_f[...].reshape(rows_f, width)
     experts_of(
         rows_f,
-        lambda: recv_f[...].reshape(rows_f, width),
+        lambda: far_rows[...],
         table[rows_n:, 1:2],
         store_far,
         sent=lambda part: each(0, lambda step: far_return(step, part).start()),
@@ -468,7 +460,7 @@
     micros, rows, width = tokens.shape
     rows_n, rows_f = half * near, half * micros * far
     vmem = pl.BlockSpec(memory_space=pltpu.VMEM)
-    block = split_columns(ff)
+    block = ff
     n_shape = (micros, half, near, width)
     f_shape = (half, micros * far, width)
     bf16 = jnp.bfloat16
@@ -485,9 +477,10 @@
             pltpu.VMEM((micros, rows, width), bf16),
             pltpu.VMEM((micros, rows_n, rows), bf16),
             pltpu.VMEM((micros, rows_f, rows), bf16),
-            pltpu.VMEM((slots * (ff // block), max(rows_n, rows_f), block), bf16),
+            pltpu.VMEM((slots * (ff // block), max(rows_n * micros, rows_f), block), bf16),
             pltpu.VMEM((micros, rows, width), bf16),
             pltpu.VMEM((micros, rows, width), jnp.float32),
+            pltpu.VMEM((rows_f, width), bf16),
             pltpu.VMEM(n_shape, bf16),
             pltpu.VMEM(f_shape, bf16),
             pltpu.VMEM(n_shape, bf16),

time: 71.1 us -> 66.9 us (0.941); the launches traced: 71 us -> 65.7 us
  Pallas kernels: 69.5 us -> 64 us
    pallas_call x1, Pallas kernels: 67.3 us -> 61.9 us  [routed(): pl.pallas_call(functools.partial(layer, near, far, slots, experts), out_s...]
where the time goes in v4:
time: 66.9 us; the launch traced here: 65.7 us
  Pallas kernels  64 us (96%)
  local copies, waits for them, and re-layouts  0.8 us (1%)
  between operations  0.67 us (1%)
    pallas_call x1, Pallas kernels, routed(): pl.pallas_call(functools.partial(layer, near, far, slots, experts), out_s...  61.9 us
    pallas_call x1, Pallas kernels, body(): pl.pallas_call(functools.partial(plan, devices, near, far, micros, expert...  2.15 us

profile of v4, /device:TPU:1, one launch (start us, length us, event | category | flops | bytes accessed | tf_op | source)
XLA Modules:
  0.0 65.7 jit_solution(6122515591039971489)
XLA Ops:
  0.0 2.2 %shard_map.84 = (s32[224,128]{1,0:T(8,128)S(1)}, s32[1]{0:T(128)}) custom-call(s32[1,32]{1,0:T(1,128)} %bitcast.26), custom_call_target="tpu_custom_call" | custom-call | tf_op jit(solution)/shard_map/pallas_call | solution.py:541
  2.8 62.1 %conditional.1 = (bf16[2,1,64,2048]{3,2,1,0:T(8,128)(2,1)S(1)}) conditional(s32[]{:T(128)} %bitcast.7, (s32[32]{0:T(128)}, bf16[2,64,2048]{2,1,0:T(8,128)(2,1)}, f32[1,2048]{1,0:T(1,128)}, s32[2,2,64]{2,1,0:T(2,128)}, f32[2,2,64]{2,1,0:T(2,128)}, /*index=5*/bf16[4,2048,768]{2,1,0:T(8,128)(2,1)}, bf16[4,2048,768]{2,1,0:T(8,128)(2,1)}, ...), branch_computations={%region_0.3_spmd, %region_3.4_spmd} | conditional | flops 9500 | bytes 209882 | solution.py:550
  2.8 61.9 %branch_1_fun.1 = bf16[2,64,2048]{2,1,0:T(8,128)(2,1)S(1)} custom-call(bf16[2,64,2048]{2,1,0:T(8,128)(2,1)} %get-tuple-element.49.tokens, f32[1,2048]{1,0:T(1,128)} %get-tuple-element.50.gain, s32[2,2,64]{2,1,0:T(2,128)} %get-tuple-element.51.ids, f32[2,2,64]{2,1,0:T(2,128)} %get-tuple-element.52.scores, s32[224,128]{1,0:T(8,128)S(1)} %get-tuple-element.53.table, ...), custom_call_target="tpu_custom_call" | custom-call | tf_op jit(solution)/shard_map/cond/branch_1_fun/pallas_call | solution.py:468
  64.9 0.8 %copy.24 = bf16[2,1,64,2048]{3,2,1,0:T(8,128)(2,1)} copy(bf16[2,1,64,2048]{3,2,1,0:T(8,128)(2,1)S(1)} %get-tuple-element.62) | data formatting | bytes 1048576

commit v5 on v4

--- a/solution.py
+++ b/solution.py
@@ -23,7 +23,7 @@
     near, far, slots, experts,
     tokens, gain, ids, scores, table, w_gate, w_up, w_down,
     out,
-    gate_buf, up_buf, down_buf, normed, hits_near, hits_far, hidden, mixed, partial, far_rows,
+    gate_buf, up_buf, down_buf, normed, hits_near, hits_far, hidden, mixed, partial, all_rows,
     send_n, send_f, recv_n, recv_f, done_n, done_f, back_n, back_f,
     weight_sem, to_n, from_n, to_f, from_f, ret_to_n, ret_from_n, ret_to_f, ret_from_f, relay_to, relay_from,
 ):
@@ -206,19 +206,7 @@
     for micro in range(micros):
         each(1, lambda step: near_copy(micro, step, send_n, recv_n, to_n, from_n).wait_recv())
 
-    def store_near(cols, value):
-        done_n[:, :, :, cols] = value.reshape(micros, half, near, value.shape[1])
-
-    experts_of(
-        rows_n * micros,
-        lambda: recv_n[...].reshape(rows_n * micros, width),
-        jnp.concatenate([table[:rows_n, 1:2]] * micros, axis=0),
-        store_near,
-        fresh=True,
-    )
-    for micro in range(micros):
-        each(1, lambda step: near_copy(micro, step, done_n, back_n, ret_to_n, ret_from_n).start())
-        back_n[micro, mine] = done_n[micro, mine]
+    all_rows[rows_f:] = recv_n[...].reshape(rows_n * micros, width)
 
     piece = width // PIECES
 
@@ -234,18 +222,23 @@
             device_id_type=MESH,
         )
 
-    def store_far(cols, value):
-        done_f[:, :, cols] = value.reshape(half, far * micros, value.shape[1])
+    def store_all(cols, value):
+        done_f[:, :, cols] = value[:rows_f].reshape(half, far * micros, value.shape[1])
+        done_n[:, :, :, cols] = value[rows_f:].reshape(micros, half, near, value.shape[1])
 
     each(0, lambda step: far_copy(step, send_f, recv_f, to_f, from_f).wait_recv())
-    far_rows[...] = recv_f[...].reshape(rows_f, width)
+    all_rows[:rows_f] = recv_f[...].reshape(rows_f, width)
     experts_of(
-        rows_f,
-        lambda: far_rows[...],
-        table[rows_n:, 1:2],
-        store_far,
+        rows_f + rows_n * micros,
+        lambda: all_rows[...],
+        jnp.concatenate([table[rows_n:, 1:2]] + [table[:rows_n, 1:2]] * micros, axis=0),
+        store_all,
+        fresh=True,
         sent=lambda part: each(0, lambda step: far_return(step, part).start()),
     )
+    for micro in range(micros):
+        each(1, lambda step: near_copy(micro, step, done_n, back_n, ret_to_n, ret_from_n).start())
+        back_n[micro, mine] = done_n[micro, mine]
 
     def weighed(mix, values):
         high = mix.astype(jnp.bfloat16)
@@ -477,10 +470,10 @@
             pltpu.VMEM((micros, rows, width), bf16),
             pltpu.VMEM((micros, rows_n, rows), bf16),
             pltpu.VMEM((micros, rows_f, rows), bf16),
-            pltpu.VMEM((slots * (ff // block), max(rows_n * micros, rows_f), block), bf16),
+            pltpu.VMEM((slots * (ff // block), rows_n * micros + rows_f, block), bf16),
             pltpu.VMEM((micros, rows, width), bf16),
             pltpu.VMEM((micros, rows, width), jnp.float32),
-            pltpu.VMEM((rows_f, width), bf16),
+            pltpu.VMEM((rows_f + rows_n * micros, width), bf16),
             pltpu.VMEM(n_shape, bf16),
             pltpu.VMEM(f_shape, bf16),
             pltpu.VMEM(n_shape, bf16),

time: 66.9 us -> 71.5 us (1.069)
  Pallas kernels: 64 us -> 69 us
    pallas_call x1, Pallas kernels: 61.9 us -> 66.9 us  [routed(): pl.pallas_call(functools.partial(layer, near, far, slots, experts), out_s...]
where the time goes in v5:
time: 71.5 us; the launch traced here: 70.5 us
  Pallas kernels  69 us (97%)
  local copies, waits for them, and re-layouts  0.8 us (1%)
    pallas_call x1, Pallas kernels, routed(): pl.pallas_call(functools.partial(layer, near, far, slots, experts), out_s...  66.9 us
    pallas_call x1, Pallas kernels, body(): pl.pallas_call(functools.partial(plan, devices, near, far, micros, expert...  2.15 us

profile of v5, /device:TPU:1, one launch (start us, length us, event | category | flops | bytes accessed | tf_op | source)
XLA Modules:
  0.0 70.5 jit_solution(11105923449057438004)
XLA Ops:
  0.0 2.2 %shard_map.84 = (s32[224,128]{1,0:T(8,128)S(1)}, s32[1]{0:T(128)}) custom-call(s32[1,32]{1,0:T(1,128)} %bitcast.26), custom_call_target="tpu_custom_call" | custom-call | tf_op jit(solution)/shard_map/pallas_call | solution.py:534
  2.8 66.9 %conditional.1 = (bf16[2,1,64,2048]{3,2,1,0:T(8,128)(2,1)S(1)}) conditional(s32[]{:T(128)} %bitcast.7, (s32[32]{0:T(128)}, bf16[2,64,2048]{2,1,0:T(8,128)(2,1)}, f32[1,2048]{1,0:T(1,128)}, s32[2,2,64]{2,1,0:T(2,128)}, f32[2,2,64]{2,1,0:T(2,128)}, /*index=5*/bf16[4,2048,768]{2,1,0:T(8,128)(2,1)}, bf16[4,2048,768]{2,1,0:T(8,128)(2,1)}, ...), branch_computations={%region_0.3_spmd, %region_3.4_spmd} | conditional | flops 9500 | bytes 209882 | solution.py:543
  2.8 66.9 %branch_1_fun.1 = bf16[2,64,2048]{2,1,0:T(8,128)(2,1)S(1)} custom-call(bf16[2,64,2048]{2,1,0:T(8,128)(2,1)} %get-tuple-element.49.tokens, f32[1,2048]{1,0:T(1,128)} %get-tuple-element.50.gain, s32[2,2,64]{2,1,0:T(2,128)} %get-tuple-element.51.ids, f32[2,2,64]{2,1,0:T(2,128)} %get-tuple-element.52.scores, s32[224,128]{1,0:T(8,128)S(1)} %get-tuple-element.53.table, ...), custom_call_target="tpu_custom_call" | custom-call | tf_op jit(solution)/shard_map/cond/branch_1_fun/pallas_call | solution.py:461
  69.7 0.8 %copy.24 = bf16[2,1,64,2048]{3,2,1,0:T(8,128)(2,1)} copy(bf16[2,1,64,2048]{3,2,1,0:T(8,128)(2,1)S(1)} %get-tuple-element.62) | data formatting | bytes 1048576
